TPU v7x, 512 devices: a whole 4x8x8 slice. The times are simulated.
512 devices in a mesh: energy: 64 (over y_hi, z, core), slab: 8 (over y_lo, x).
Axes of the slice: x: 4, y: 8 (y_hi: 4, y_lo: 2; y = y_hi * 2 + y_lo), z: 8, core: 2. Of those that a mesh axis runs over, the one named last changes fastest.
Arguments:
- green: bfloat16 [64, 32, 512, 512], P('energy', 'slab'), may hold values from -6 to 6
- coupling: bfloat16 [32, 3, 512, 512], P('slab'), may hold values from -0.25 to 0.25
- bonds: int32 [32, 3], P('slab'), may hold values from 0 to 31, as said below
- counts: int32 [64], P('energy'), may hold values from 1 to 32
- bose: float32 [1], replicated, may hold values from 0.3 to 2
Outputs:
- sigma: bfloat16 [64, 32, 512, 512], P('energy', 'slab')
Inputs may be any that keep to these rules, and one draw needn't show every extreme that they name: `bonds`: the first bond of a block reaches the block itself; the other two reach the block just before or just after it, different blocks where both exist, else both the single neighbour.
All inputs are finite; a program needn't handle non-finite values.
Results may differ from a plain program's by a relative error of at most 0.0057.
Values may be sent and summed in bfloat16 or wider, within the bound.
A program may use at most 64 MiB of HBM per device.

v0:
```python
import jax
import jax.numpy as jnp
from jax import lax
from jax.sharding import PartitionSpec as P

OFF = 8


def extended_2(value, sides, width):
    for axis, dim in sides:
        size, length = (lax.axis_size(axis), value.shape[dim])
        up = [(i, (i + 1) % size) for i in range(size - 1)]
        down = [(j, i) for i, j in up]
        last = lax.slice_in_dim(value, length - width, length, axis=dim)
        initial = lax.slice_in_dim(value, 0, width, axis=dim)
        before = lax.ppermute(last, axis, up)
        after = lax.ppermute(initial, axis, down)
        value = jnp.concatenate([before, value, after], axis=dim)
    return value


def shifted(block, axis, distance):
    devices = range(lax.axis_size(axis))
    route = [(i - distance, i) for i in devices if i - distance in devices]
    return lax.ppermute(block, axis, route)


def triples(extended, coupling, local):
    e_count = extended.shape[0]
    b_count = local.shape[0]
    k_count = local.shape[1]
    orbitals = extended.shape[-1]
    near = jnp.take(extended, local.reshape(-1), axis=1).reshape(
        e_count, b_count, k_count, orbitals, orbitals
    )
    left = jnp.einsum(
        "bkij,ebkjl->ebkil", coupling, near, preferred_element_type=jnp.float32
    ).astype(jnp.bfloat16)
    part = jnp.einsum("ebkil,bkml->ebim", left, coupling, preferred_element_type=jnp.float32)
    return part.astype(jnp.bfloat16)


def on_device(green, coupling, bonds, counts, bose):
    e_count = green.shape[0]
    b_count = green.shape[1]
    hops = OFF // e_count
    extended = extended_2(green, (("slab", 1),), 1)
    first_block = lax.axis_index("slab") * b_count
    local = bonds - first_block + 1
    part = triples(extended, coupling, local)
    above = shifted(part, "energy", -hops)
    below = shifted(part, "energy", hops)
    occupation = bose[0]
    block_ids = first_block + jnp.arange(b_count, dtype=jnp.int32)
    active = (block_ids[None, :] < counts[:, None]).astype(jnp.float32)
    total = (occupation + 1.0) * above.astype(jnp.float32) + occupation * below.astype(jnp.float32)
    return (total * active[:, :, None, None]).astype(jnp.bfloat16)


def solution(mesh):
    in_specs = (
        P("energy", "slab", None, None),
        P("slab", None, None, None),
        P("slab", None),
        P("energy"),
        P(),
    )
    out_specs = P("energy", "slab", None, None)
    return jax.shard_map(
        on_device, mesh=mesh, in_specs=in_specs, out_specs=out_specs, check_vma=False
    )
```

profile of v0, /device:TPU:22, one launch (start us, length us, event | category | flops | bytes accessed | tf_op | source)
XLA Modules:
  0.0 249.4 jit_solution(9908718252438715303)
XLA Ops:
  0.0 1.3 fusion.20
  1.3 3.4 %collective-permute-start = (bf16[1,1,512,512]{3,2,1,0:T(8,128)(2,1)S(1)}, bf16[1,1,512,512]{3,2,1,0:T(8,128)(2,1)S(1)}, u32[]{:S(2)}, u32[]{:S(2)}) collective-permute-start(bf16[1,1,512,512]{3,2,1,0:T(8,128)(2,1)S(1)} %get-tuple-element.5), channel_id=1, source_target_pairs={{0,1},{1,2},{2,3},{3,4},{4,5},{5,6},{6,7},{8,9},{9,10},{10,11},{11... | collective-permute-start | bytes 1572872 | tf_op jit(solution)/shard_map/ppermute | solution.py:16
  4.7 2.4 collective-permute-start.1
  7.1 0.7 subtract_add_fusion
  7.8 0.1 reshape.65
  7.9 0.7 compare_and_fusion
  8.6 8.2 %collective-permute-done = bf16[1,1,512,512]{3,2,1,0:T(8,128)(2,1)S(1)} collective-permute-done((bf16[1,1,512,512]{3,2,1,0:T(8,128)(2,1)S(1)}, bf16[1,1,512,512]{3,2,1,0:T(8,128)(2,1)S(1)}, u32[]{:S(2)}, u32[]{:S(2)}) %collective-permute-start) | collective-permute-done | bytes 524320 | tf_op jit(solution)/shard_map/ppermute | solution.py:16
  16.8 0.0 copy-start
  16.8 0.8 copy-done
  17.6 4.5 %collective-permute-done.1 = bf16[1,1,512,512]{3,2,1,0:T(8,128)(2,1)} collective-permute-done((bf16[1,1,512,512]{3,2,1,0:T(8,128)(2,1)S(1)}, bf16[1,1,512,512]{3,2,1,0:T(8,128)(2,1)}, u32[]{:S(2)}, u32[]{:S(2)}) %collective-permute-start.1) | collective-permute-done | bytes 524320 | tf_op jit(solution)/shard_map/ppermute | solution.py:17
  22.2 2.2 maximum_bitcast_fusion
  24.4 4.2 %gather_fusion = bf16[12,512,512]{2,1,0:T(8,128)(2,1)} fusion(bf16[6,512,512]{2,1,0:T(8,128)(2,1)S(1)} %maximum_bitcast_fusion, s32[1024]{0:T(1024)S(1)} %pad_clamp_fusion), kind=kCustom, calls=%fused_computation | custom fusion | bytes 12582960 | tf_op jit(solution)/shard_map/jit(_take)/gather | solution.py:33
  28.6 8.7 %copy.6 = bf16[4,3,512,512]{2,3,1,0:T(8,128)(2,1)} copy(bf16[4,3,512,512]{3,2,1,0:T(8,128)(2,1)} %bitcast.32) | data formatting | bytes 12582912 | tf_op jit(solution)/shard_map/jit(_take)/gather | solution.py:33
  37.2 14.3 %fusion.12 = bf16[1,4,512,512]{3,2,1,0:T(8,128)(2,1)} fusion(bf16[4,3,512,512]{3,2,1,0:T(8,128)(2,1)} %param.6, bf16[4,3,512,512]{2,3,1,0:T(8,128)(2,1)} %copy.6, pred[4,3]{1,0:T(4,128)(4,1)S(1)} %compare_and_fusion), kind=kOutput, calls=%fused_computation.11 | convolution fusion | flops 6449790976 | bytes 14680076 | tf_op jit(solution)/shard_map/ebkil,bkml->ebim/dot_general | solution.py:39
  51.5 10.7 %collective-permute-start.2 = (bf16[1,4,512,512]{3,2,1,0:T(8,128)(2,1)}, bf16[1,4,512,512]{3,2,1,0:T(8,128)(2,1)S(1)}, u32[]{:S(2)}, u32[]{:S(2)}) collective-permute-start(bf16[1,4,512,512]{3,2,1,0:T(8,128)(2,1)} %fusion.12), channel_id=1, source_target_pairs={{64,0},{72,8},{80,16},{88,24},{96,32},{104,40},{112,48},{120,56},{... | collective-permute-start | bytes 6291464 | tf_op jit(solution)/shard_map/ppermute | solution.py:25
  62.2 2.2 collective-permute-start.3
  65.7 171.9 %collective-permute-done.2 = bf16[1,4,512,512]{3,2,1,0:T(8,128)(2,1)S(1)} collective-permute-done((bf16[1,4,512,512]{3,2,1,0:T(8,128)(2,1)}, bf16[1,4,512,512]{3,2,1,0:T(8,128)(2,1)S(1)}, u32[]{:S(2)}, u32[]{:S(2)}) %collective-permute-start.2) | collective-permute-done | bytes 2097184 | tf_op jit(solution)/shard_map/ppermute | solution.py:25
  237.6 7.9 %collective-permute-done.3 = bf16[1,4,512,512]{3,2,1,0:T(8,128)(2,1)} collective-permute-done((bf16[1,4,512,512]{3,2,1,0:T(8,128)(2,1)}, bf16[1,4,512,512]{3,2,1,0:T(8,128)(2,1)}, u32[]{:S(2)}, u32[]{:S(2)}) %collective-permute-start.3) | collective-permute-done | bytes 2097184 | tf_op jit(solution)/shard_map/ppermute | solution.py:25
  245.5 3.9 %multiply_convert_fusion = bf16[1,4,512,512]{3,2,1,0:T(8,128)(2,1)} fusion(bf16[1,4,512,512]{3,2,1,0:T(8,128)(2,1)} %collective-permute-done.3, bf16[1,4,512,512]{3,2,1,0:T(8,128)(2,1)S(1)} %collective-permute-done.2, f32[4]{0:T(128)S(1)} %compare_convert_fusion, f32[]{:T(128)} %bitcast.31, f32[]{:T(128)S(6)} %add.40), kind=kLoop, calls=%fused_computation.8 | loop fusion | flops 7340032 | bytes 6291480 | tf_op jit(solution)/shard_map/convert_element_type | solution.py:57
  (3 shorter events, 0.0 us)
Async XLA Ops:
  1.3 15.6 %collective-permute-start = (bf16[1,1,512,512]{3,2,1,0:T(8,128)(2,1)S(1)}, bf16[1,1,512,512]{3,2,1,0:T(8,128)(2,1)S(1)}, u32[]{:S(2)}, u32[]{:S(2)}) collective-permute-start(bf16[1,1,512,512]{3,2,1,0:T(8,128)(2,1)S(1)} %get-tuple-element.5), channel_id=1, source_target_pairs={{0,1},{1,2},{2,3},{3,4},{4,5},{5,6},{6,7},{8,9},{9,10},{10,11},{11... | collective-permute-start | bytes 1572872 | tf_op jit(solution)/shard_map/ppermute | solution.py:16
  4.7 17.5 %collective-permute-start.1 = (bf16[1,1,512,512]{3,2,1,0:T(8,128)(2,1)S(1)}, bf16[1,1,512,512]{3,2,1,0:T(8,128)(2,1)}, u32[]{:S(2)}, u32[]{:S(2)}) collective-permute-start(bf16[1,1,512,512]{3,2,1,0:T(8,128)(2,1)S(1)} %get-tuple-element.6), channel_id=1, source_target_pairs={{1,0},{2,1},{3,2},{4,3},{5,4},{6,5},{7,6},{9,8},{10,9},{11,10},{12... | collective-permute-start | bytes 1572872 | tf_op jit(solution)/shard_map/ppermute | solution.py:17
  16.8 0.8 copy-start
  51.5 186.1 %collective-permute-start.2 = (bf16[1,4,512,512]{3,2,1,0:T(8,128)(2,1)}, bf16[1,4,512,512]{3,2,1,0:T(8,128)(2,1)S(1)}, u32[]{:S(2)}, u32[]{:S(2)}) collective-permute-start(bf16[1,4,512,512]{3,2,1,0:T(8,128)(2,1)} %fusion.12), channel_id=1, source_target_pairs={{64,0},{72,8},{80,16},{88,24},{96,32},{104,40},{112,48},{120,56},{... | collective-permute-start | bytes 6291464 | tf_op jit(solution)/shard_map/ppermute | solution.py:25
  62.2 183.3 %collective-permute-start.3 = (bf16[1,4,512,512]{3,2,1,0:T(8,128)(2,1)}, bf16[1,4,512,512]{3,2,1,0:T(8,128)(2,1)}, u32[]{:S(2)}, u32[]{:S(2)}) collective-permute-start(bf16[1,4,512,512]{3,2,1,0:T(8,128)(2,1)} %fusion.12), channel_id=1, source_target_pairs={{0,64},{8,72},{16,80},{24,88},{32,96},{40,104},{48,112},{56,120},{... | collective-permute-start | bytes 6291464 | tf_op jit(solution)/shard_map/ppermute | solution.py:25
where the time goes:
time: 250 us; the launch traced here: 249 us
  waiting for transfers between devices  193 us (77%)
  starting transfers between devices  18.7 us (7%)
  local copies, waits for them, and re-layouts  15 us (6%)
  matrix products  14.3 us (6%)
  other arithmetic  7.49 us (3%)
    ppermute x2, waiting for transfers between devices, shifted(): return lax.ppermute(block, axis, route)  180 us
    dot_general x1, matrix products, triples(): jnp.einsum('ebkil,bkml->ebim', left, coupling, preferred_element_type=jnp...  14.3 us
    gather x2, local copies, waits for them, and re-layouts, triples(): jnp.take(extended, local.reshape(-1), axis=1)  12.9 us
    ppermute x2, starting transfers between devices, shifted(): return lax.ppermute(block, axis, route)  12.8 us
    ppermute x1, waiting for transfers between devices, extended_2(): before = lax.ppermute(last, axis, up)  8.21 us
  transfers between devices with their start and end apart: 4, of which 4 were waited for; matrix products, arithmetic and copies ran while one was open for 1% of the time, Pallas kernels for 0%

commit v1 on v0

v1 whole, which is shorter than its diff:
```python
import functools

import jax
import jax.numpy as jnp
from jax import lax
from jax.experimental import pallas as pl
from jax.experimental.pallas import tpu as pltpu
from jax.sharding import PartitionSpec as P

OFF = 8
MESH = pl.DeviceIdType.MESH
MIB = 2**20


def kernel(
    energies, slabs, rows,
    green, coupling, bonds, counts, bose, sigma,
    g, before, after, c0, c1, c2, c3,
    part_z, part_y, got_z, got_q, got_y, sig_z, sig_own, cnt_own, cnt_got,
    load_sem, halo_send, halo_recv, cnt_sem,
    z_send, z_recv, q_send, q_recv, y_send, y_recv, o_send, o_recv, w_sem,
):
    e = lax.axis_index("energy")
    s = lax.axis_index("slab")
    orb = g.shape[-1]
    tiles = orb // rows
    n_tiles = 2 * tiles
    upper = (e // OFF) % 2
    partner = e + OFF - 2 * OFF * upper
    up = (e + 2 * OFF) % energies
    down = (e + energies - 2 * OFF) % energies
    y_to = jnp.where(upper == 0, down, up)
    q_to = jnp.where(upper == 0, up, down)
    left = (s + slabs - 1) % slabs
    right = (s + 1) % slabs

    barrier = pltpu.get_barrier_semaphore()
    for device in ((partner, s), (up, s), (down, s), (e, left), (e, right)):
        pl.semaphore_signal(barrier, inc=1, device_id=device, device_id_type=MESH)

    blocks = (c0, c1, c2, c3)
    loads = [pltpu.make_async_copy(green.at[0], g, load_sem.at[4])]
    loads += [pltpu.make_async_copy(coupling.at[b], blocks[b], load_sem.at[b]) for b in range(4)]
    for i in (0, 2, 3, 1, 4):
        loads[i].start()

    cnt_own[...] = jnp.full(cnt_own.shape, counts[0], jnp.int32)

    def remote(src, dst, send, recv, device):
        return pltpu.make_async_remote_copy(
            src_ref=src, dst_ref=dst, send_sem=send, recv_sem=recv,
            device_id=device, device_id_type=MESH,
        )

    to_right = remote(green.at[0, 3], before, halo_send.at[0], halo_recv.at[0], (e, right))
    to_left = remote(green.at[0, 0], after, halo_send.at[1], halo_recv.at[1], (e, left))
    edge_before = pltpu.make_async_copy(green.at[0, 1], before, halo_recv.at[0])
    edge_after = pltpu.make_async_copy(green.at[0, 2], after, halo_recv.at[1])
    count = remote(cnt_own, cnt_got, cnt_sem.at[0], cnt_sem.at[1], (partner, s))

    def place(i):
        return i // tiles, pl.ds(pl.multiple_of((i % tiles) * rows, rows), rows)

    def z_copy(i):
        j, r = place(i)
        return remote(part_z.at[j, r], got_z.at[j, r], z_send.at[i], z_recv.at[i], (partner, s))

    def q_copy(i):
        j, r = place(i)
        return remote(got_z.at[j, r], got_q.at[j, r], q_send.at[i], q_recv.at[i], (q_to, s))

    def y_copy(i):
        j, r = place(i)
        return remote(part_y.at[j, r], got_y.at[j, r], y_send.at[i], y_recv.at[i], (y_to, s))

    def o_copy(i):
        j, r = place(i)
        return remote(sig_z.at[j, r], sigma.at[0, 3 * j, r], o_send.at[i], o_recv.at[i], (partner, s))

    def w_copy(i):
        j, r = place(i)
        return pltpu.make_async_copy(sig_own.at[j, r], sigma.at[0, 1 + j, r], w_sem.at[i])

    def products(b, r, lower, higher):
        c = blocks[b]
        k = 1 + (bonds[b, 1] > bonds[b, 0]).astype(jnp.int32)
        total = None
        for k, near in ((0, g.at[b]), (k, lower), (3 - k, higher)):
            half = jnp.dot(c[k, r, :], near[...], preferred_element_type=jnp.float32)
            term = lax.dot_general(
                half.astype(jnp.bfloat16), c[k], (((1,), (1,)), ((), ())),
                preferred_element_type=jnp.float32,
            )
            total = term if total is None else total + term
        return total.astype(jnp.bfloat16)

    loads[0].wait()
    for j in (0, 1):
        loads[2 + j].wait()

        def inner(t, _, j=j):
            i = j * tiles + t
            _, r = place(i)
            part_z[j, r, :] = products(1 + j, r, g.at[j], g.at[2 + j])

            if j == 0:
                @pl.when(t == 0)
                def _():
                    pl.semaphore_wait(barrier, 5)

                    @pl.when(s < slabs - 1)
                    def _():
                        to_right.start()

                    @pl.when(s > 0)
                    def _():
                        to_left.start()

                    count.start()

            z_copy(i).start()
            return 0

        lax.fori_loop(0, tiles, inner, 0)

    @pl.when(s == 0)
    def _():
        edge_before.start()

    @pl.when(s == slabs - 1)
    def _():
        edge_after.start()

    for j, (lower, higher, edge, b) in enumerate(
        ((before, g.at[1], to_right, 0), (g.at[2], after, to_left, 3))
    ):
        edge.wait_recv()
        loads[1 if b == 0 else 4].wait()

        def outer(t, _, j=j, lower=lower, higher=higher, b=b):
            i = j * tiles + t
            _, r = place(i)
            part_y[j, r, :] = products(b, r, lower, higher)
            y_copy(i).start()
            return 0

        lax.fori_loop(0, tiles, outer, 0)

    n = bose[0]
    has_up = e + 2 * OFF < energies
    has_down = e >= 2 * OFF
    y_own = jnp.where(upper == 0, n, n + 1.0)
    y_far = jnp.where(upper == 0, jnp.where(has_up, n + 1.0, 0.0), jnp.where(has_down, n, 0.0))
    q_own = jnp.where(upper == 0, n + 1.0, n)
    q_far = jnp.where(upper == 0, jnp.where(has_down, n, 0.0), jnp.where(has_up, n + 1.0, 0.0))
    count.wait_recv()

    def combine(own, far, own_factor, far_factor, cnt, block):
        active = cnt[0:1, :] > block
        total = own_factor * own.astype(jnp.float32) + far_factor * far.astype(jnp.float32)
        return jnp.where(active, total, 0.0).astype(jnp.bfloat16)

    def middle(i, _):
        j, r = place(i)
        z_copy(i).wait_recv()
        q_copy(i).start()
        y_copy(i).wait_recv()
        sig_z[j, r, :] = combine(part_y[j, r, :], got_y[j, r, :], y_own, y_far, cnt_got, s * 4 + 3 * j)
        o_copy(i).start()
        return 0

    lax.fori_loop(0, n_tiles, middle, 0)

    def last(i, _):
        j, r = place(i)
        q_copy(i).wait_recv()
        sig_own[j, r, :] = combine(got_z[j, r, :], got_q[j, r, :], q_own, q_far, cnt_own, s * 4 + 1 + j)
        w_copy(i).start()
        return 0

    lax.fori_loop(0, n_tiles, last, 0)

    @pl.when(s < slabs - 1)
    def _():
        to_right.wait_send()

    @pl.when(s > 0)
    def _():
        to_left.wait_send()

    count.wait_send()

    def finish(i, _):
        z_copy(i).wait_send()
        q_copy(i).wait_send()
        y_copy(i).wait_send()
        o_copy(i).wait_send()
        w_copy(i).wait()
        o_copy(i).wait_recv()
        return 0

    lax.fori_loop(0, n_tiles, finish, 0)


def solution(mesh):
    energies, slabs = mesh.shape["energy"], mesh.shape["slab"]

    def on_device(green, coupling, bonds, counts, bose):
        orb = green.shape[-1]
        rows = 128
        n_tiles = 2 * (orb // rows)
        block = (orb, orb)
        dma = pltpu.SemaphoreType.DMA
        pair = pltpu.VMEM((2,) + block, jnp.bfloat16)
        hbm = pl.BlockSpec(memory_space=pl.ANY)
        smem = pl.BlockSpec(memory_space=pltpu.SMEM)
        return pl.pallas_call(
            functools.partial(kernel, energies, slabs, rows),
            out_shape=jax.ShapeDtypeStruct(green.shape, jnp.bfloat16),
            in_specs=[hbm, hbm, smem, smem, smem],
            out_specs=hbm,
            scratch_shapes=[
                pltpu.VMEM((4,) + block, jnp.bfloat16),
                pltpu.VMEM(block, jnp.bfloat16),
                pltpu.VMEM(block, jnp.bfloat16),
            ]
            + [pltpu.VMEM((3,) + block, jnp.bfloat16)] * 4
            + [pair] * 7
            + [pltpu.VMEM((8, orb), jnp.int32)] * 2
            + [dma((5,)), dma((2,)), dma((2,)), dma((2,))]
            + [dma((n_tiles,))] * 9,
            compiler_params=pltpu.CompilerParams(
                collective_id=0, has_side_effects=True, vmem_limit_bytes=60 * MIB
            ),
            cost_estimate=pl.CostEstimate(
                flops=48 * orb**3, bytes_accessed=20 * MIB, transcendentals=0
            ),
            name="self_energy",
        )(green, coupling, bonds, counts, bose)

    return jax.shard_map(
        on_device,
        mesh=mesh,
        in_specs=(
            P("energy", "slab", None, None),
            P("slab", None, None, None),
            P("slab", None),
            P("energy"),
            P(),
        ),
        out_specs=P("energy", "slab", None, None),
        check_vma=False,
    )
```

time: 250 us -> 115 us (0.46)
  the two profiles are of different devices: /device:TPU:22 before, /device:TPU:10 now
where the time goes in v1:
time: 115 us; the launch traced here: 114 us
  Pallas kernels  110 us (96%)
  local copies, waits for them, and re-layouts  3.05 us (3%)
  between operations  1.3 us (1%)
    pallas_call x1, Pallas kernels, on_device(): pl.pallas_call(functools.partial(kernel, energies, slabs, rows), out_shap...  110 us
    unnamed x1, local copies, waits for them, and re-layouts  3.05 us

profile of v1, /device:TPU:10, one launch (start us, length us, event | category | flops | bytes accessed | tf_op | source)
XLA Modules:
  0.0 114.4 jit_solution(2051704881065826736)
XLA Ops:
  1.3 110.0 %self_energy.1 = bf16[1,4,512,512]{3,2,1,0:T(8,128)(2,1)} custom-call(bf16[1,4,512,512]{3,2,1,0:T(8,128)(2,1)} %green.1, bf16[4,3,512,512]{3,2,1,0:T(8,128)(2,1)} %coupling.1, s32[4,3]{1,0:T(4,128)} %bonds.1, s32[1]{0:T(128)S(6)} %copy.7.counts, f32[1]{0:T(128)S(6)} %copy.8.bose), custom_call_target="tpu_custom_call" | custom-call | flops 6442450944 | bytes 20971520 | tf_op jit(solution)/shard_map/self_energy/pallas_call | solution.py:217
  111.3 3.0 %copy.9 = bf16[1,4,512,512]{3,2,1,0:T(8,128)(2,1)} copy(bf16[1,4,512,512]{3,2,1,0:T(8,128)(2,1)} %self_energy.1) | data formatting | bytes 4194304

commit v2 on v1

v2 whole, which is shorter than its diff:
```python
import functools

import jax
import jax.numpy as jnp
from jax import lax
from jax.experimental import pallas as pl
from jax.experimental.pallas import tpu as pltpu
from jax.sharding import PartitionSpec as P

OFF = 8
ROWS = 128
MESH = pl.DeviceIdType.MESH
MIB = 2**20
ORDER = (1, 2, 0, 3)


def kernel(
    energies, slabs,
    green, coupling, bonds_hbm, counts_hbm, bose_hbm, sigma,
    g, before, after, c0, c1, c2, c3,
    part, got_z, got_q, got_y, sig, cnt_own, cnt_got, bonds, counts, bose,
    load_sem, small_sem, halo_send, halo_recv, cnt_sem, y_ok, q_ok,
    z_send, z_recv, q_send, q_recv, y_send, y_recv, o_send, o_recv,
):
    e = lax.axis_index("energy")
    s = lax.axis_index("slab")
    orb = g.shape[-1]
    per = orb // ROWS
    upper = (e // OFF) % 2
    late = (e // 4) % 2 == 1
    early = jnp.logical_not(late)
    partner = e + OFF - 2 * OFF * upper
    up = (e + 2 * OFF) % energies
    down = (e + energies - 2 * OFF) % energies
    y_to = jnp.where(upper == 0, down, up)
    q_to = jnp.where(upper == 0, up, down)
    left = (s + slabs - 1) % slabs
    right = (s + 1) % slabs

    barrier = pltpu.get_barrier_semaphore()
    peers = [(partner, s), (up, s), (down, s), (e, left), (e, right)]
    for device in peers:
        pl.semaphore_signal(barrier, inc=1, device_id=device, device_id_type=MESH)

    blocks = (c0, c1, c2, c3)
    small = [
        pltpu.make_async_copy(src, dst, small_sem.at[i])
        for i, (src, dst) in enumerate(((bonds_hbm, bonds), (counts_hbm, counts), (bose_hbm, bose)))
    ]
    for copy in small:
        copy.start()
    load_g = [pltpu.make_async_copy(green.at[0, b], g.at[b], load_sem.at[b]) for b in range(4)]
    load_c = [pltpu.make_async_copy(coupling.at[b], blocks[b], load_sem.at[4 + b]) for b in range(4)]
    for copy in (load_g[1], load_c[1], load_g[0], load_g[2], load_c[2], load_g[3], load_c[0], load_c[3]):
        copy.start()
    for copy in small:
        copy.wait()
    cnt_own[...] = jnp.full(cnt_own.shape, counts[0], jnp.int32)

    def remote(src, dst, send, recv, device):
        return pltpu.make_async_remote_copy(
            src_ref=src, dst_ref=dst, send_sem=send, recv_sem=recv,
            device_id=device, device_id_type=MESH,
        )

    to_right = remote(green.at[0, 3], before, halo_send.at[0], halo_recv.at[0], (e, right))
    to_left = remote(green.at[0, 0], after, halo_send.at[1], halo_recv.at[1], (e, left))
    edge_before = pltpu.make_async_copy(green.at[0, 1], before, halo_recv.at[0])
    edge_after = pltpu.make_async_copy(green.at[0, 2], after, halo_recv.at[1])
    count = remote(cnt_own, cnt_got, cnt_sem.at[0], cnt_sem.at[1], (partner, s))

    def rows_of(t):
        return t // per, pl.ds(pl.multiple_of((t % per) * ROWS, ROWS), ROWS)

    def block_of(j):
        return jnp.where(j < 2, j + 1, jnp.where(j == 2, 0, 3))

    def z_copy(t):
        j, r = rows_of(t)
        return remote(part.at[j, r], got_z.at[j, r], z_send.at[t], z_recv.at[t], (partner, s))

    def q_copy(t):
        j, r = rows_of(t)
        return remote(got_z.at[j, r], got_q.at[j, r], q_send.at[t], q_recv.at[t], (q_to, s))

    def y_copy(t):
        j, r = rows_of(t)
        return remote(part.at[j, r], got_y.at[j, r], y_send.at[t], y_recv.at[t], (y_to, s))

    def o_copy(t):
        j, r = rows_of(t)
        return remote(sig.at[j, r], sigma.at[0, block_of(j), r], o_send.at[t], o_recv.at[t], (partner, s))

    def z_first(t):
        return jnp.where(early, t // per != 2, t // per == 3)

    def when(flag, action):
        @pl.when(flag)
        def _():
            action()

    def loop(first, last, body):
        def step(t, _):
            body(t)
            return 0

        lax.fori_loop(first, last, step, 0)

    def products(b, r, lower, higher):
        c = blocks[b]
        k = 1 + (bonds[b, 1] > bonds[b, 0]).astype(jnp.int32)
        total = None
        for k, near in ((0, g.at[b]), (k, lower), (3 - k, higher)):
            half = jnp.dot(c[k, r, :], near[...], preferred_element_type=jnp.float32)
            term = lax.dot_general(
                half.astype(jnp.bfloat16), c[k], (((1,), (1,)), ((), ())),
                preferred_element_type=jnp.float32,
            )
            total = term if total is None else total + term
        return total.astype(jnp.bfloat16)

    def first_sends():
        pl.semaphore_wait(barrier, len(peers))
        when(s < slabs - 1, to_right.start)
        when(s > 0, to_left.start)
        count.start()

    def work(j, lower, higher):
        def tile(t):
            _, r = rows_of(t)
            part[j, r, :] = products(ORDER[j], r, lower, higher)
            if j == 0:
                when(t == 0, first_sends)
            if j == 2:
                y_copy(t).start()
            else:
                when(early, z_copy(t).start)

        loop(j * per, (j + 1) * per, tile)

    def forward(t):
        z_copy(t).wait_recv()
        q_copy(t).start()

    for b in (1, 0, 2):
        load_g[b].wait()
    load_c[1].wait()
    work(0, g.at[0], g.at[2])
    load_g[3].wait()
    load_c[2].wait()
    work(1, g.at[1], g.at[3])
    when(s == 0, edge_before.start)
    when(s == slabs - 1, edge_after.start)
    to_right.wait_recv()
    to_left.wait_recv()
    pl.semaphore_signal(y_ok, inc=1, device_id=(q_to, s), device_id_type=MESH)
    pl.semaphore_signal(q_ok, inc=1, device_id=(y_to, s), device_id_type=MESH)
    pl.semaphore_wait(y_ok, 1)
    pl.semaphore_wait(q_ok, 1)
    when(late, lambda: loop(0, 2 * per, lambda t: y_copy(t).start()))
    when(early, lambda: loop(0, 3, forward))
    load_c[0].wait()
    work(2, before, g.at[1])
    load_c[3].wait()
    work(3, g.at[2], after)

    n = bose[0]
    has_up = e + 2 * OFF < energies
    has_down = e >= 2 * OFF
    y_own = jnp.where(upper == 0, n, n + 1.0)
    y_far = jnp.where(upper == 0, jnp.where(has_up, n + 1.0, 0.0), jnp.where(has_down, n, 0.0))
    q_own = jnp.where(upper == 0, n + 1.0, n)
    q_far = jnp.where(upper == 0, jnp.where(has_down, n, 0.0), jnp.where(has_up, n + 1.0, 0.0))

    def combine(own, far, own_factor, far_factor, cnt, block):
        active = cnt[0:1, :] > block
        total = own_factor * own.astype(jnp.float32) + far_factor * far.astype(jnp.float32)
        return jnp.where(active, total, 0.0).astype(jnp.bfloat16)

    def across(t):
        j, r = rows_of(t)
        y_copy(t).wait_recv()
        sig[j, r, :] = combine(part[j, r, :], got_y[j, r, :], y_own, y_far, cnt_got, s * 4 + block_of(j))
        o_copy(t).start()

    count.wait_recv()
    period = 2 * per

    def early_part():
        loop(3, 8, forward)
        loop(8, 10, across)
        loop(12, 14, forward)
        loop(10, 12, across)
        loop(14, 16, forward)

    def late_part():
        loop(12, 16, lambda t: z_copy(t).start())
        loop(0, 6, across)
        loop(12, 14, forward)
        loop(6, 8, across)
        loop(14, 16, forward)
        loop(8, 12, across)

    when(early, early_part)
    when(late, late_part)

    def own(t):
        def action():
            j, r = rows_of(t)
            q_copy(t).wait_recv()
            sigma[0, block_of(j), r, :] = combine(
                got_z[j, r, :], got_q[j, r, :], q_own, q_far, cnt_own, s * 4 + block_of(j)
            )

        when(z_first(t), action)

    loop(0, 2 * period, own)

    when(s < slabs - 1, to_right.wait_send)
    when(s > 0, to_left.wait_send)
    count.wait_send()

    def finish(t):
        def z_way():
            z_copy(t).wait_send()
            q_copy(t).wait_send()

        def y_way():
            y_copy(t).wait_send()
            o_copy(t).wait_send()
            o_copy(t).wait_recv()

        when(z_first(t), z_way)
        when(jnp.logical_not(z_first(t)), y_way)

    loop(0, 2 * period, finish)


def solution(mesh):
    energies, slabs = mesh.shape["energy"], mesh.shape["slab"]

    def on_device(green, coupling, bonds, counts, bose):
        orb = green.shape[-1]
        tiles = 4 * (orb // ROWS)
        block = (orb, orb)
        dma = pltpu.SemaphoreType.DMA
        whole = pltpu.VMEM((4,) + block, jnp.bfloat16)
        hbm = pl.BlockSpec(memory_space=pltpu.HBM)
        return pl.pallas_call(
            functools.partial(kernel, energies, slabs),
            out_shape=pltpu.VMEM(green.shape, jnp.bfloat16),
            in_specs=[hbm] * 5,
            out_specs=pl.BlockSpec(memory_space=pltpu.VMEM),
            scratch_shapes=[
                whole,
                pltpu.VMEM(block, jnp.bfloat16),
                pltpu.VMEM(block, jnp.bfloat16),
            ]
            + [pltpu.VMEM((3,) + block, jnp.bfloat16)] * 4
            + [whole] * 5
            + [pltpu.VMEM((8, orb), jnp.int32)] * 2
            + [pltpu.SMEM(bonds.shape, jnp.int32), pltpu.SMEM((1,), jnp.int32), pltpu.SMEM((1,), jnp.float32)]
            + [dma((8,)), dma((3,)), dma((2,)), dma((2,)), dma((2,))] + [pltpu.SemaphoreType.REGULAR] * 2
            + [dma((tiles,))] * 8,
            compiler_params=pltpu.CompilerParams(
                collective_id=0, has_side_effects=True, vmem_limit_bytes=60 * MIB
            ),
            cost_estimate=pl.CostEstimate(
                flops=48 * orb**3, bytes_accessed=20 * MIB, transcendentals=0
            ),
            name="self_energy",
        )(green, coupling, bonds, counts, bose)

    return jax.shard_map(
        on_device,
        mesh=mesh,
        in_specs=(
            P("energy", "slab", None, None),
            P("slab", None, None, None),
            P("slab", None),
            P("energy"),
            P(),
        ),
        out_specs=P("energy", "slab", None, None),
        check_vma=False,
    )
```

time: 115 us -> 107 us (0.930)
  the two profiles are of different devices: /device:TPU:10 before, /device:TPU:129 now
where the time goes in v2:
time: 107 us
  Pallas kernels  105 us (98%)
  local copies, waits for them, and re-layouts  1.32 us (1%)
  between operations  1.3 us (1%)
    pallas_call x1, Pallas kernels, on_device(): pl.pallas_call(functools.partial(kernel, energies, slabs), out_shape=pltp...  105 us

profile of v2, /device:TPU:129, one launch (start us, length us, event | category | flops | bytes accessed | tf_op | source)
XLA Modules:
  0.0 107.3 jit_solution(15313405442256732274)
XLA Ops:
  1.3 104.7 %self_energy.1 = bf16[1,4,512,512]{3,2,1,0:T(8,128)(2,1)S(1)} custom-call(bf16[1,4,512,512]{3,2,1,0:T(8,128)(2,1)} %green.1, bf16[4,3,512,512]{3,2,1,0:T(8,128)(2,1)} %coupling.1, s32[4,3]{1,0:T(4,128)} %bonds_hbm.1, s32[1]{0:T(128)S(6)} %copy.8.counts_hbm, f32[1]{0:T(128)S(6)} %copy.9.bose_hbm), custom_call_target="tpu_custom_call" | custom-call | flops 6442450944 | bytes 20971520 | tf_op jit(solution)/shard_map/self_energy/pallas_call | solution.py:249
  106.0 1.3 %copy.7 = bf16[1,4,512,512]{3,2,1,0:T(8,128)(2,1)} copy(bf16[1,4,512,512]{3,2,1,0:T(8,128)(2,1)S(1)} %self_energy.1) | data formatting | bytes 4194304

commit v3 on v2

--- a/solution.py
+++ b/solution.py
@@ -51,7 +51,7 @@
         copy.start()
     load_g = [pltpu.make_async_copy(green.at[0, b], g.at[b], load_sem.at[b]) for b in range(4)]
     load_c = [pltpu.make_async_copy(coupling.at[b], blocks[b], load_sem.at[4 + b]) for b in range(4)]
-    for copy in (load_g[1], load_c[1], load_g[0], load_g[2], load_c[2], load_g[3], load_c[0], load_c[3]):
+    for copy in (load_g[1], load_c[1], load_g[0], load_g[2]):
         copy.start()
     for copy in small:
         copy.wait()
@@ -92,7 +92,7 @@
         return remote(sig.at[j, r], sigma.at[0, block_of(j), r], o_send.at[t], o_recv.at[t], (partner, s))
 
     def z_first(t):
-        return jnp.where(early, t // per != 2, t // per == 3)
+        return jnp.where(early, t // per != 2, t // per == 0)
 
     def when(flag, action):
         @pl.when(flag)
@@ -131,10 +131,14 @@
             part[j, r, :] = products(ORDER[j], r, lower, higher)
             if j == 0:
                 when(t == 0, first_sends)
-            if j == 2:
+            if j == 0:
+                z_copy(t).start()
+            elif j == 2:
                 y_copy(t).start()
             else:
                 when(early, z_copy(t).start)
+                if j == 3:
+                    when(late, y_copy(t).start)
 
         loop(j * per, (j + 1) * per, tile)
 
@@ -145,6 +149,8 @@
     for b in (1, 0, 2):
         load_g[b].wait()
     load_c[1].wait()
+    for copy in (load_c[2], load_g[3], load_c[0], load_c[3]):
+        copy.start()
     work(0, g.at[0], g.at[2])
     load_g[3].wait()
     load_c[2].wait()
@@ -157,7 +163,7 @@
     pl.semaphore_signal(q_ok, inc=1, device_id=(y_to, s), device_id_type=MESH)
     pl.semaphore_wait(y_ok, 1)
     pl.semaphore_wait(q_ok, 1)
-    when(late, lambda: loop(0, 2 * per, lambda t: y_copy(t).start()))
+    when(late, lambda: loop(per, 2 * per, lambda t: y_copy(t).start()))
     when(early, lambda: loop(0, 3, forward))
     load_c[0].wait()
     work(2, before, g.at[1])
@@ -194,12 +200,9 @@
         loop(14, 16, forward)
 
     def late_part():
-        loop(12, 16, lambda t: z_copy(t).start())
-        loop(0, 6, across)
-        loop(12, 14, forward)
-        loop(6, 8, across)
-        loop(14, 16, forward)
-        loop(8, 12, across)
+        loop(0, 2, forward)
+        loop(2, 4, lambda t: (across(t + 2), forward(t)))
+        loop(6, 16, across)
 
     when(early, early_part)
     when(late, late_part)

time: 107 us -> 107 us (level)
  no operation moved by 1% of the time
where the time goes in v3:
time: 107 us
  Pallas kernels  105 us (98%)
  local copies, waits for them, and re-layouts  1.32 us (1%)
  between operations  1.3 us (1%)
    pallas_call x1, Pallas kernels, on_device(): pl.pallas_call(functools.partial(kernel, energies, slabs), out_shape=pltp...  105 us

profile of v3, /device:TPU:129, one launch (start us, length us, event | category | flops | bytes accessed | tf_op | source)
XLA Modules:
  0.0 107.3 jit_solution(17179687655753808873)
XLA Ops:
  1.3 104.7 %self_energy.1 = bf16[1,4,512,512]{3,2,1,0:T(8,128)(2,1)S(1)} custom-call(bf16[1,4,512,512]{3,2,1,0:T(8,128)(2,1)} %green.1, bf16[4,3,512,512]{3,2,1,0:T(8,128)(2,1)} %coupling.1, s32[4,3]{1,0:T(4,128)} %bonds_hbm.1, s32[1]{0:T(128)S(6)} %copy.8.counts_hbm, f32[1]{0:T(128)S(6)} %copy.9.bose_hbm), custom_call_target="tpu_custom_call" | custom-call | flops 6442450944 | bytes 20971520 | tf_op jit(solution)/shard_map/self_energy/pallas_call | solution.py:252
  106.0 1.3 %copy.7 = bf16[1,4,512,512]{3,2,1,0:T(8,128)(2,1)} copy(bf16[1,4,512,512]{3,2,1,0:T(8,128)(2,1)S(1)} %self_energy.1) | data formatting | bytes 4194304

commit v4 on v3

--- a/solution.py
+++ b/solution.py
@@ -37,10 +37,29 @@
     left = (s + slabs - 1) % slabs
     right = (s + 1) % slabs
 
+    has_up = e + 2 * OFF < energies
+    has_down = e >= 2 * OFF
+    has_left = s > 0
+    has_right = s < slabs - 1
+    y_in = jnp.where(upper == 0, has_up, has_down)
+    y_out = jnp.where(upper == 0, has_down, has_up)
+    q_in, q_out = y_out, y_in
+
+    def when(flag, action):
+        @pl.when(flag)
+        def _():
+            action()
+
+    def signal(semaphore, device):
+        pl.semaphore_signal(semaphore, inc=1, device_id=device, device_id_type=MESH)
+
     barrier = pltpu.get_barrier_semaphore()
-    peers = [(partner, s), (up, s), (down, s), (e, left), (e, right)]
-    for device in peers:
-        pl.semaphore_signal(barrier, inc=1, device_id=device, device_id_type=MESH)
+    signal(barrier, (partner, s))
+    for flag, device in (
+        (has_up, (up, s)), (has_down, (down, s)), (has_left, (e, left)), (has_right, (e, right)),
+    ):
+        when(flag, lambda device=device: signal(barrier, device))
+    n_peers = 1 + sum(flag.astype(jnp.int32) for flag in (has_up, has_down, has_left, has_right))
 
     blocks = (c0, c1, c2, c3)
     small = [
@@ -94,11 +113,6 @@
     def z_first(t):
         return jnp.where(early, t // per != 2, t // per == 0)
 
-    def when(flag, action):
-        @pl.when(flag)
-        def _():
-            action()
-
     def loop(first, last, body):
         def step(t, _):
             body(t)
@@ -120,9 +134,9 @@
         return total.astype(jnp.bfloat16)
 
     def first_sends():
-        pl.semaphore_wait(barrier, len(peers))
-        when(s < slabs - 1, to_right.start)
-        when(s > 0, to_left.start)
+        pl.semaphore_wait(barrier, n_peers)
+        when(has_right, to_right.start)
+        when(has_left, to_left.start)
         count.start()
 
     def work(j, lower, higher):
@@ -134,17 +148,17 @@
             if j == 0:
                 z_copy(t).start()
             elif j == 2:
-                y_copy(t).start()
+                when(y_out, y_copy(t).start)
             else:
                 when(early, z_copy(t).start)
                 if j == 3:
-                    when(late, y_copy(t).start)
+                    when(jnp.logical_and(late, y_out), y_copy(t).start)
 
         loop(j * per, (j + 1) * per, tile)
 
     def forward(t):
         z_copy(t).wait_recv()
-        q_copy(t).start()
+        when(q_out, q_copy(t).start)
 
     for b in (1, 0, 2):
         load_g[b].wait()
@@ -159,11 +173,11 @@
     when(s == slabs - 1, edge_after.start)
     to_right.wait_recv()
     to_left.wait_recv()
-    pl.semaphore_signal(y_ok, inc=1, device_id=(q_to, s), device_id_type=MESH)
-    pl.semaphore_signal(q_ok, inc=1, device_id=(y_to, s), device_id_type=MESH)
-    pl.semaphore_wait(y_ok, 1)
-    pl.semaphore_wait(q_ok, 1)
-    when(late, lambda: loop(per, 2 * per, lambda t: y_copy(t).start()))
+    when(y_in, lambda: signal(y_ok, (q_to, s)))
+    when(q_in, lambda: signal(q_ok, (y_to, s)))
+    when(y_out, lambda: pl.semaphore_wait(y_ok, 1))
+    when(q_out, lambda: pl.semaphore_wait(q_ok, 1))
+    when(jnp.logical_and(late, y_out), lambda: loop(per, 2 * per, lambda t: y_copy(t).start()))
     when(early, lambda: loop(0, 3, forward))
     load_c[0].wait()
     work(2, before, g.at[1])
@@ -171,22 +185,24 @@
     work(3, g.at[2], after)
 
     n = bose[0]
-    has_up = e + 2 * OFF < energies
-    has_down = e >= 2 * OFF
-    y_own = jnp.where(upper == 0, n, n + 1.0)
-    y_far = jnp.where(upper == 0, jnp.where(has_up, n + 1.0, 0.0), jnp.where(has_down, n, 0.0))
-    q_own = jnp.where(upper == 0, n + 1.0, n)
-    q_far = jnp.where(upper == 0, jnp.where(has_down, n, 0.0), jnp.where(has_up, n + 1.0, 0.0))
-
-    def combine(own, far, own_factor, far_factor, cnt, block):
-        active = cnt[0:1, :] > block
-        total = own_factor * own.astype(jnp.float32) + far_factor * far.astype(jnp.float32)
-        return jnp.where(active, total, 0.0).astype(jnp.bfloat16)
+    y_own, y_far = jnp.where(upper == 0, n, n + 1.0), jnp.where(upper == 0, n + 1.0, n)
+    q_own, q_far = y_far, y_own
+
+    def combine(target, terms, cnt, block):
+        total = sum(factor * value.astype(jnp.float32) for factor, value in terms)
+        target[...] = jnp.where(cnt[0:1, :] > block, total, 0.0).astype(jnp.bfloat16)
 
     def across(t):
         j, r = rows_of(t)
-        y_copy(t).wait_recv()
-        sig[j, r, :] = combine(part[j, r, :], got_y[j, r, :], y_own, y_far, cnt_got, s * 4 + block_of(j))
+        own = (y_own, part[j, r, :])
+        block = s * 4 + block_of(j)
+
+        def both():
+            y_copy(t).wait_recv()
+            combine(sig.at[j, r], (own, (y_far, got_y[j, r, :])), cnt_got, block)
+
+        when(y_in, both)
+        when(jnp.logical_not(y_in), lambda: combine(sig.at[j, r], (own,), cnt_got, block))
         o_copy(t).start()
 
     count.wait_recv()
@@ -207,29 +223,31 @@
     when(early, early_part)
     when(late, late_part)
 
-    def own(t):
-        def action():
-            j, r = rows_of(t)
+    def keep(t):
+        j, r = rows_of(t)
+        target = sigma.at[0, block_of(j), r]
+        block = s * 4 + block_of(j)
+
+        def both():
             q_copy(t).wait_recv()
-            sigma[0, block_of(j), r, :] = combine(
-                got_z[j, r, :], got_q[j, r, :], q_own, q_far, cnt_own, s * 4 + block_of(j)
-            )
-
-        when(z_first(t), action)
-
-    loop(0, 2 * period, own)
-
-    when(s < slabs - 1, to_right.wait_send)
-    when(s > 0, to_left.wait_send)
+            combine(target, ((q_own, got_z[j, r, :]), (q_far, got_q[j, r, :])), cnt_own, block)
+
+        when(q_in, both)
+        when(jnp.logical_not(q_in), lambda: combine(target, ((q_own, got_z[j, r, :]),), cnt_own, block))
+
+    loop(0, 2 * period, lambda t: when(z_first(t), lambda: keep(t)))
+
+    when(has_right, to_right.wait_send)
+    when(has_left, to_left.wait_send)
     count.wait_send()
 
     def finish(t):
         def z_way():
             z_copy(t).wait_send()
-            q_copy(t).wait_send()
+            when(q_out, q_copy(t).wait_send)
 
         def y_way():
-            y_copy(t).wait_send()
+            when(y_out, y_copy(t).wait_send)
             o_copy(t).wait_send()
             o_copy(t).wait_recv()
 

time: 107 us -> 108 us (level)
  the two profiles are of different devices: /device:TPU:129 before, /device:TPU:249 now
where the time goes in v4:
time: 108 us; the launch traced here: 107 us
  Pallas kernels  105 us (97%)
  local copies, waits for them, and re-layouts  1.32 us (1%)
  between operations  1.3 us (1%)
    pallas_call x1, Pallas kernels, on_device(): pl.pallas_call(functools.partial(kernel, energies, slabs), out_shape=pltp...  105 us

profile of v4, /device:TPU:249, one launch (start us, length us, event | category | flops | bytes accessed | tf_op | source)
XLA Modules:
  0.0 107.4 jit_solution(10266204494206375939)
XLA Ops:
  1.3 104.8 %self_energy.1 = bf16[1,4,512,512]{3,2,1,0:T(8,128)(2,1)S(1)} custom-call(bf16[1,4,512,512]{3,2,1,0:T(8,128)(2,1)} %green.1, bf16[4,3,512,512]{3,2,1,0:T(8,128)(2,1)} %coupling.1, s32[4,3]{1,0:T(4,128)} %bonds_hbm.1, s32[1]{0:T(128)S(6)} %copy.8.counts_hbm, f32[1]{0:T(128)S(6)} %copy.9.bose_hbm), custom_call_target="tpu_custom_call" | custom-call | flops 6442450944 | bytes 20971520 | tf_op jit(solution)/shard_map/self_energy/pallas_call | solution.py:270
  106.1 1.3 %copy.7 = bf16[1,4,512,512]{3,2,1,0:T(8,128)(2,1)} copy(bf16[1,4,512,512]{3,2,1,0:T(8,128)(2,1)S(1)} %self_energy.1) | data formatting | bytes 4194304

commit v5 on v4

--- a/solution.py
+++ b/solution.py
@@ -12,6 +12,7 @@
 MESH = pl.DeviceIdType.MESH
 MIB = 2**20
 ORDER = (1, 2, 0, 3)
+CHUNK = (256, 512, 512, 512)
 
 
 def kernel(
@@ -139,22 +140,19 @@
         when(has_left, to_left.start)
         count.start()
 
-    def work(j, lower, higher):
-        def tile(t):
-            _, r = rows_of(t)
+    def work(j, lower, higher, send=None):
+        rows = CHUNK[j]
+
+        def chunk(i):
+            r = pl.ds(pl.multiple_of(i * rows, rows), rows)
             part[j, r, :] = products(ORDER[j], r, lower, higher)
             if j == 0:
-                when(t == 0, first_sends)
-            if j == 0:
-                z_copy(t).start()
-            elif j == 2:
-                when(y_out, y_copy(t).start)
-            else:
-                when(early, z_copy(t).start)
-                if j == 3:
-                    when(jnp.logical_and(late, y_out), y_copy(t).start)
-
-        loop(j * per, (j + 1) * per, tile)
+                when(i == 0, first_sends)
+            if send is not None:
+                first = j * per + i * (rows // ROWS)
+                loop(first, first + rows // ROWS, send)
+
+        loop(0, orb // rows, chunk)
 
     def forward(t):
         z_copy(t).wait_recv()
@@ -165,24 +163,27 @@
     load_c[1].wait()
     for copy in (load_c[2], load_g[3], load_c[0], load_c[3]):
         copy.start()
-    work(0, g.at[0], g.at[2])
+    work(0, g.at[0], g.at[2], lambda t: z_copy(t).start())
     load_g[3].wait()
     load_c[2].wait()
-    work(1, g.at[1], g.at[3])
+    work(1, g.at[1], g.at[3], lambda t: when(early, z_copy(t).start))
     when(s == 0, edge_before.start)
     when(s == slabs - 1, edge_after.start)
     to_right.wait_recv()
     to_left.wait_recv()
     when(y_in, lambda: signal(y_ok, (q_to, s)))
     when(q_in, lambda: signal(q_ok, (y_to, s)))
+    load_c[0].wait()
+    work(2, before, g.at[1])
     when(y_out, lambda: pl.semaphore_wait(y_ok, 1))
     when(q_out, lambda: pl.semaphore_wait(q_ok, 1))
     when(jnp.logical_and(late, y_out), lambda: loop(per, 2 * per, lambda t: y_copy(t).start()))
+    when(y_out, lambda: loop(2 * per, 3 * per, lambda t: y_copy(t).start()))
     when(early, lambda: loop(0, 3, forward))
-    load_c[0].wait()
-    work(2, before, g.at[1])
     load_c[3].wait()
-    work(3, g.at[2], after)
+    work(3, g.at[2], after, lambda t: (
+        when(early, z_copy(t).start), when(jnp.logical_and(late, y_out), y_copy(t).start)
+    ))
 
     n = bose[0]
     y_own, y_far = jnp.where(upper == 0, n, n + 1.0), jnp.where(upper == 0, n + 1.0, n)

time: 108 us -> 108 us (level)
  no operation moved by 1% of the time
where the time goes in v5:
time: 108 us; the launch traced here: 107 us
  Pallas kernels  105 us (97%)
  local copies, waits for them, and re-layouts  1.32 us (1%)
  between operations  1.3 us (1%)
    pallas_call x1, Pallas kernels, on_device(): pl.pallas_call(functools.partial(kernel, energies, slabs), out_shape=pltp...  105 us

profile of v5, /device:TPU:249, one launch (start us, length us, event | category | flops | bytes accessed | tf_op | source)
XLA Modules:
  0.0 107.4 jit_solution(3240434349557149413)
XLA Ops:
  1.3 104.8 %self_energy.1 = bf16[1,4,512,512]{3,2,1,0:T(8,128)(2,1)S(1)} custom-call(bf16[1,4,512,512]{3,2,1,0:T(8,128)(2,1)} %green.1, bf16[4,3,512,512]{3,2,1,0:T(8,128)(2,1)} %coupling.1, s32[4,3]{1,0:T(4,128)} %bonds_hbm.1, s32[1]{0:T(128)S(6)} %copy.8.counts_hbm, f32[1]{0:T(128)S(6)} %copy.9.bose_hbm), custom_call_target="tpu_custom_call" | custom-call | flops 6442450944 | bytes 20971520 | tf_op jit(solution)/shard_map/self_energy/pallas_call | solution.py:271
  106.1 1.3 %copy.7 = bf16[1,4,512,512]{3,2,1,0:T(8,128)(2,1)} copy(bf16[1,4,512,512]{3,2,1,0:T(8,128)(2,1)S(1)} %self_energy.1) | data formatting | bytes 4194304

commit v6 on v5

--- a/solution.py
+++ b/solution.py
@@ -12,7 +12,7 @@
 MESH = pl.DeviceIdType.MESH
 MIB = 2**20
 ORDER = (1, 2, 0, 3)
-CHUNK = (256, 512, 512, 512)
+CHUNK = (128, 512, 512, 512)
 
 
 def kernel(
@@ -171,19 +171,17 @@
     when(s == slabs - 1, edge_after.start)
     to_right.wait_recv()
     to_left.wait_recv()
+    load_c[0].wait()
+    work(2, before, g.at[1])
     when(y_in, lambda: signal(y_ok, (q_to, s)))
     when(q_in, lambda: signal(q_ok, (y_to, s)))
-    load_c[0].wait()
-    work(2, before, g.at[1])
+    load_c[3].wait()
+    work(3, g.at[2], after, lambda t: when(early, z_copy(t).start))
     when(y_out, lambda: pl.semaphore_wait(y_ok, 1))
     when(q_out, lambda: pl.semaphore_wait(q_ok, 1))
-    when(jnp.logical_and(late, y_out), lambda: loop(per, 2 * per, lambda t: y_copy(t).start()))
-    when(y_out, lambda: loop(2 * per, 3 * per, lambda t: y_copy(t).start()))
+    when(jnp.logical_and(late, y_out), lambda: loop(per, 4 * per, lambda t: y_copy(t).start()))
+    when(jnp.logical_and(early, y_out), lambda: loop(2 * per, 3 * per, lambda t: y_copy(t).start()))
     when(early, lambda: loop(0, 3, forward))
-    load_c[3].wait()
-    work(3, g.at[2], after, lambda t: (
-        when(early, z_copy(t).start), when(jnp.logical_and(late, y_out), y_copy(t).start)
-    ))
 
     n = bose[0]
     y_own, y_far = jnp.where(upper == 0, n, n + 1.0), jnp.where(upper == 0, n + 1.0, n)

time: 108 us -> 108 us (level)
  no operation moved by 1% of the time
where the time goes in v6:
time: 108 us
  Pallas kernels  105 us (97%)
  local copies, waits for them, and re-layouts  1.32 us (1%)
  between operations  1.3 us (1%)
    pallas_call x1, Pallas kernels, on_device(): pl.pallas_call(functools.partial(kernel, energies, slabs), out_shape=pltp...  105 us

profile of v6, /device:TPU:249, one launch (start us, length us, event | category | flops | bytes accessed | tf_op | source)
XLA Modules:
  0.0 107.5 jit_solution(15572034019435474062)
XLA Ops:
  1.3 104.9 %self_energy.1 = bf16[1,4,512,512]{3,2,1,0:T(8,128)(2,1)S(1)} custom-call(bf16[1,4,512,512]{3,2,1,0:T(8,128)(2,1)} %green.1, bf16[4,3,512,512]{3,2,1,0:T(8,128)(2,1)} %coupling.1, s32[4,3]{1,0:T(4,128)} %bonds_hbm.1, s32[1]{0:T(128)S(6)} %copy.8.counts_hbm, f32[1]{0:T(128)S(6)} %copy.9.bose_hbm), custom_call_target="tpu_custom_call" | custom-call | flops 6442450944 | bytes 20971520 | tf_op jit(solution)/shard_map/self_energy/pallas_call | solution.py:269
  106.2 1.3 %copy.7 = bf16[1,4,512,512]{3,2,1,0:T(8,128)(2,1)} copy(bf16[1,4,512,512]{3,2,1,0:T(8,128)(2,1)S(1)} %self_energy.1) | data formatting | bytes 4194304

commit v7 on v5

--- a/solution.py
+++ b/solution.py
@@ -12,7 +12,7 @@
 MESH = pl.DeviceIdType.MESH
 MIB = 2**20
 ORDER = (1, 2, 0, 3)
-CHUNK = (256, 512, 512, 512)
+CHUNK = (128, 512, 512, 512)
 
 
 def kernel(
@@ -179,7 +179,6 @@
     when(q_out, lambda: pl.semaphore_wait(q_ok, 1))
     when(jnp.logical_and(late, y_out), lambda: loop(per, 2 * per, lambda t: y_copy(t).start()))
     when(y_out, lambda: loop(2 * per, 3 * per, lambda t: y_copy(t).start()))
-    when(early, lambda: loop(0, 3, forward))
     load_c[3].wait()
     work(3, g.at[2], after, lambda t: (
         when(early, z_copy(t).start), when(jnp.logical_and(late, y_out), y_copy(t).start)
@@ -210,16 +209,16 @@
     period = 2 * per
 
     def early_part():
-        loop(3, 8, forward)
+        loop(0, 6, forward)
         loop(8, 10, across)
-        loop(12, 14, forward)
+        loop(6, 8, forward)
         loop(10, 12, across)
-        loop(14, 16, forward)
+        loop(12, 16, forward)
 
     def late_part():
-        loop(0, 2, forward)
-        loop(2, 4, lambda t: (across(t + 2), forward(t)))
-        loop(6, 16, across)
+        loop(4, 8, across)
+        loop(0, 4, forward)
+        loop(8, 16, across)
 
     when(early, early_part)
     when(late, late_part)

time: 108 us -> 108 us (level)
  no operation moved by 1% of the time
where the time goes in v7:
time: 108 us; the launch traced here: 107 us
  Pallas kernels  105 us (97%)
  local copies, waits for them, and re-layouts  1.32 us (1%)
  between operations  1.3 us (1%)
    pallas_call x1, Pallas kernels, on_device(): pl.pallas_call(functools.partial(kernel, energies, slabs), out_shape=pltp...  105 us

profile of v7, /device:TPU:249, one launch (start us, length us, event | category | flops | bytes accessed | tf_op | source)
XLA Modules:
  0.0 107.4 jit_solution(5849179682023204634)
XLA Ops:
  1.3 104.8 %self_energy.1 = bf16[1,4,512,512]{3,2,1,0:T(8,128)(2,1)S(1)} custom-call(bf16[1,4,512,512]{3,2,1,0:T(8,128)(2,1)} %green.1, bf16[4,3,512,512]{3,2,1,0:T(8,128)(2,1)} %coupling.1, s32[4,3]{1,0:T(4,128)} %bonds_hbm.1, s32[1]{0:T(128)S(6)} %copy.8.counts_hbm, f32[1]{0:T(128)S(6)} %copy.9.bose_hbm), custom_call_target="tpu_custom_call" | custom-call | flops 6442450944 | bytes 20971520 | tf_op jit(solution)/shard_map/self_energy/pallas_call | solution.py:270
  106.1 1.3 %copy.7 = bf16[1,4,512,512]{3,2,1,0:T(8,128)(2,1)} copy(bf16[1,4,512,512]{3,2,1,0:T(8,128)(2,1)S(1)} %self_energy.1) | data formatting | bytes 4194304

commit v8 on v5

--- a/solution.py
+++ b/solution.py
@@ -12,7 +12,7 @@
 MESH = pl.DeviceIdType.MESH
 MIB = 2**20
 ORDER = (1, 2, 0, 3)
-CHUNK = (256, 512, 512, 512)
+CHUNK = (128, 512, 512, 512)
 
 
 def kernel(
@@ -20,7 +20,7 @@
     green, coupling, bonds_hbm, counts_hbm, bose_hbm, sigma,
     g, before, after, c0, c1, c2, c3,
     part, got_z, got_q, got_y, sig, cnt_own, cnt_got, bonds, counts, bose,
-    load_sem, small_sem, halo_send, halo_recv, cnt_sem, y_ok, q_ok,
+    load_sem, first_sem, small_sem, halo_send, halo_recv, cnt_sem, y_ok, q_ok,
     z_send, z_recv, q_send, q_recv, y_send, y_recv, o_send, o_recv,
 ):
     e = lax.axis_index("energy")
@@ -70,12 +70,10 @@
     for copy in small:
         copy.start()
     load_g = [pltpu.make_async_copy(green.at[0, b], g.at[b], load_sem.at[b]) for b in range(4)]
-    load_c = [pltpu.make_async_copy(coupling.at[b], blocks[b], load_sem.at[4 + b]) for b in range(4)]
-    for copy in (load_g[1], load_c[1], load_g[0], load_g[2]):
+    load_c = {b: pltpu.make_async_copy(coupling.at[b], blocks[b], load_sem.at[4 + b]) for b in (0, 2, 3)}
+    early_c = [pltpu.make_async_copy(coupling.at[1, k], c1.at[k], first_sem.at[k]) for k in range(3)]
+    for copy in (load_g[1], early_c[0], load_g[0], early_c[1], early_c[2], load_g[2]):
         copy.start()
-    for copy in small:
-        copy.wait()
-    cnt_own[...] = jnp.full(cnt_own.shape, counts[0], jnp.int32)
 
     def remote(src, dst, send, recv, device):
         return pltpu.make_async_remote_copy(
@@ -121,49 +119,59 @@
 
         lax.fori_loop(first, last, step, 0)
 
-    def products(b, r, lower, higher):
+    def term(c, k, r, near):
+        half = jnp.dot(c[k, r, :], near[...], preferred_element_type=jnp.float32)
+        return lax.dot_general(
+            half.astype(jnp.bfloat16), c[k], (((1,), (1,)), ((), ())),
+            preferred_element_type=jnp.float32,
+        )
+
+    def products(b, r, lower, higher, ready=None):
         c = blocks[b]
+        total = term(c, 0, r, g.at[b])
+        if ready is not None:
+            ready()
         k = 1 + (bonds[b, 1] > bonds[b, 0]).astype(jnp.int32)
-        total = None
-        for k, near in ((0, g.at[b]), (k, lower), (3 - k, higher)):
-            half = jnp.dot(c[k, r, :], near[...], preferred_element_type=jnp.float32)
-            term = lax.dot_general(
-                half.astype(jnp.bfloat16), c[k], (((1,), (1,)), ((), ())),
-                preferred_element_type=jnp.float32,
-            )
-            total = term if total is None else total + term
+        total = total + term(c, k, r, lower)
+        total = total + term(c, 3 - k, r, higher)
         return total.astype(jnp.bfloat16)
 
+    def rest():
+        for copy in small + early_c[1:] + [load_g[0], load_g[2]]:
+            copy.wait()
+        for copy in (load_c[2], load_g[3], load_c[0], load_c[3]):
+            copy.start()
+
     def first_sends():
-        pl.semaphore_wait(barrier, n_peers)
+        cnt_own[...] = jnp.full(cnt_own.shape, counts[0], jnp.int32)
         when(has_right, to_right.start)
         when(has_left, to_left.start)
         count.start()
 
-    def work(j, lower, higher, send=None):
+    def work(j, lower, higher, send=None, start=0):
         rows = CHUNK[j]
 
         def chunk(i):
             r = pl.ds(pl.multiple_of(i * rows, rows), rows)
             part[j, r, :] = products(ORDER[j], r, lower, higher)
-            if j == 0:
-                when(i == 0, first_sends)
             if send is not None:
                 first = j * per + i * (rows // ROWS)
                 loop(first, first + rows // ROWS, send)
 
-        loop(0, orb // rows, chunk)
+        loop(start, orb // rows, chunk)
 
     def forward(t):
         z_copy(t).wait_recv()
         when(q_out, q_copy(t).start)
 
-    for b in (1, 0, 2):
-        load_g[b].wait()
-    load_c[1].wait()
-    for copy in (load_c[2], load_g[3], load_c[0], load_c[3]):
-        copy.start()
-    work(0, g.at[0], g.at[2], lambda t: z_copy(t).start())
+    load_g[1].wait()
+    early_c[0].wait()
+    top = pl.ds(0, CHUNK[0])
+    part[0, top, :] = products(1, top, g.at[0], g.at[2], rest)
+    pl.semaphore_wait(barrier, n_peers)
+    loop(0, CHUNK[0] // ROWS, lambda t: z_copy(t).start())
+    first_sends()
+    work(0, g.at[0], g.at[2], lambda t: z_copy(t).start(), 1)
     load_g[3].wait()
     load_c[2].wait()
     work(1, g.at[1], g.at[3], lambda t: when(early, z_copy(t).start))
@@ -282,7 +290,7 @@
             + [whole] * 5
             + [pltpu.VMEM((8, orb), jnp.int32)] * 2
             + [pltpu.SMEM(bonds.shape, jnp.int32), pltpu.SMEM((1,), jnp.int32), pltpu.SMEM((1,), jnp.float32)]
-            + [dma((8,)), dma((3,)), dma((2,)), dma((2,)), dma((2,))] + [pltpu.SemaphoreType.REGULAR] * 2
+            + [dma((8,)), dma((3,)), dma((3,)), dma((2,)), dma((2,)), dma((2,))] + [pltpu.SemaphoreType.REGULAR] * 2
             + [dma((tiles,))] * 8,
             compiler_params=pltpu.CompilerParams(
                 collective_id=0, has_side_effects=True, vmem_limit_bytes=60 * MIB

time: 108 us -> 108 us (level)
  no operation moved by 1% of the time
where the time goes in v8:
time: 108 us; the launch traced here: 107 us
  Pallas kernels  105 us (97%)
  local copies, waits for them, and re-layouts  1.32 us (1%)
  between operations  1.3 us (1%)
    pallas_call x1, Pallas kernels, on_device(): pl.pallas_call(functools.partial(kernel, energies, slabs), out_shape=pltp...  105 us

profile of v8, /device:TPU:249, one launch (start us, length us, event | category | flops | bytes accessed | tf_op | source)
XLA Modules:
  0.0 107.5 jit_solution(13996947729244687538)
XLA Ops:
  1.3 104.8 %self_energy.1 = bf16[1,4,512,512]{3,2,1,0:T(8,128)(2,1)S(1)} custom-call(bf16[1,4,512,512]{3,2,1,0:T(8,128)(2,1)} %green.1, bf16[4,3,512,512]{3,2,1,0:T(8,128)(2,1)} %coupling.1, s32[4,3]{1,0:T(4,128)} %bonds_hbm.1, s32[1]{0:T(128)S(6)} %copy.8.counts_hbm, f32[1]{0:T(128)S(6)} %copy.9.bose_hbm), custom_call_target="tpu_custom_call" | custom-call | flops 6442450944 | bytes 20971520 | tf_op jit(solution)/shard_map/self_energy/pallas_call | solution.py:279
  106.1 1.3 %copy.7 = bf16[1,4,512,512]{3,2,1,0:T(8,128)(2,1)} copy(bf16[1,4,512,512]{3,2,1,0:T(8,128)(2,1)S(1)} %self_energy.1) | data formatting | bytes 4194304

commit v9 on v8

--- a/solution.py
+++ b/solution.py
@@ -187,7 +187,6 @@
     when(q_out, lambda: pl.semaphore_wait(q_ok, 1))
     when(jnp.logical_and(late, y_out), lambda: loop(per, 2 * per, lambda t: y_copy(t).start()))
     when(y_out, lambda: loop(2 * per, 3 * per, lambda t: y_copy(t).start()))
-    when(early, lambda: loop(0, 3, forward))
     load_c[3].wait()
     work(3, g.at[2], after, lambda t: (
         when(early, z_copy(t).start), when(jnp.logical_and(late, y_out), y_copy(t).start)
@@ -218,16 +217,16 @@
     period = 2 * per
 
     def early_part():
-        loop(3, 8, forward)
+        loop(0, 6, forward)
         loop(8, 10, across)
-        loop(12, 14, forward)
+        loop(6, 8, forward)
         loop(10, 12, across)
-        loop(14, 16, forward)
+        loop(12, 16, forward)
 
     def late_part():
-        loop(0, 2, forward)
-        loop(2, 4, lambda t: (across(t + 2), forward(t)))
-        loop(6, 16, across)
+        loop(4, 8, across)
+        loop(0, 4, forward)
+        loop(8, 16, across)
 
     when(early, early_part)
     when(late, late_part)

time: 108 us -> 108 us (level)
  no operation moved by 1% of the time
where the time goes in v9:
time: 108 us; the launch traced here: 107 us
  Pallas kernels  105 us (97%)
  local copies, waits for them, and re-layouts  1.32 us (1%)
  between operations  1.3 us (1%)
    pallas_call x1, Pallas kernels, on_device(): pl.pallas_call(functools.partial(kernel, energies, slabs), out_shape=pltp...  105 us

profile of v9, /device:TPU:249, one launch (start us, length us, event | category | flops | bytes accessed | tf_op | source)
XLA Modules:
  0.0 107.5 jit_solution(12025463361608550874)
XLA Ops:
  1.3 104.8 %self_energy.1 = bf16[1,4,512,512]{3,2,1,0:T(8,128)(2,1)S(1)} custom-call(bf16[1,4,512,512]{3,2,1,0:T(8,128)(2,1)} %green.1, bf16[4,3,512,512]{3,2,1,0:T(8,128)(2,1)} %coupling.1, s32[4,3]{1,0:T(4,128)} %bonds_hbm.1, s32[1]{0:T(128)S(6)} %copy.8.counts_hbm, f32[1]{0:T(128)S(6)} %copy.9.bose_hbm), custom_call_target="tpu_custom_call" | custom-call | flops 6442450944 | bytes 20971520 | tf_op jit(solution)/shard_map/self_energy/pallas_call | solution.py:278
  106.1 1.3 %copy.7 = bf16[1,4,512,512]{3,2,1,0:T(8,128)(2,1)} copy(bf16[1,4,512,512]{3,2,1,0:T(8,128)(2,1)S(1)} %self_energy.1) | data formatting | bytes 4194304
